TPU v7x, 256 devices: a whole 4x4x8 slice. The times are simulated.
256 devices in a mesh: row: 8 (over y, core), col: 32 (over z, x).
Axes of the slice: x: 4, y: 4, z: 8, core: 2. Of those that a mesh axis runs over, the one named last changes fastest.
Arguments:
- cotangent: bfloat16 [8192, 4096], P('col'), may hold values from -600 to 600
- token_ids: int32 [8192], replicated, may hold values from 0 to 31999, as said below
- param: float32 [32000, 4096], P('row', 'col'), may hold values from -14 to 14
- row_moment: float32 [32000], P('row'), may hold values from 1 to 120
- col_moment: float32 [4096], P('col'), may hold values from 0.1 to 1
Outputs:
- new_param: float32 [32000, 4096], P('row', 'col')
- update: float32 [32000, 4096], P('row', 'col')
- new_row: float32 [32000], P('row')
- new_col: float32 [4096], P('col')
- row_factor: float32 [32000], P('row')
Inputs may be any that keep to these rules, and one draw needn't show every extreme that they name: `token_ids`: in each aligned block of 256 tokens, at most 64 ids lie in any one range of 4000 vocabulary rows starting at a multiple of 4000, and some range holds exactly 64.
All inputs are finite; a program needn't handle non-finite values.
Results may differ from a plain program's by a relative error of at most 0.0003.
Values may be sent and summed in bfloat16 or wider, within the bound.
A program may use at most 64 MiB of HBM per device.

v0:
```python
import jax
import jax.numpy as jnp
from jax import lax
from jax.sharding import PartitionSpec as P

V = 32000
D = 4096
STEP = 100


def body(cotangent, token_ids, param, row_moment, col_moment):
    row_index = lax.axis_index("row")
    local_rows = param.shape[0]
    first_row = row_index * local_rows
    decay = 1.0 - STEP ** (-0.8)
    rate = min(0.01, STEP ** (-0.5))
    cells = float(V) * float(D)
    param_total = lax.psum(jnp.sum(param * param), ("row", "col"))
    arrived = lax.all_to_all(cotangent, "col", split_axis=1, concat_axis=0, tiled=True)
    filled = jnp.ones(token_ids.shape, jnp.bool_)
    local_row = token_ids - first_row
    inside = filled & (local_row >= 0) & (local_row < local_rows)
    contrib = jnp.where(inside[:, None], arrived.astype(jnp.float32), 0.0)
    targets = jnp.where(inside, local_row, 0)
    gradient = jax.ops.segment_sum(contrib, targets, num_segments=local_rows)
    squared = gradient * gradient + 1e-30
    row_local = jnp.sum(squared, axis=1)
    col_local = jnp.sum(squared, axis=0)
    col_total = lax.psum(col_local, "row")
    new_col = decay * col_moment + (1.0 - decay) * (col_total / V)
    row_total = lax.psum(row_local, "col")
    new_row = decay * row_moment + (1.0 - decay) * (row_total / D)
    mean_row = lax.psum(jnp.sum(new_row), "row") / V
    row_factor = lax.rsqrt(new_row / mean_row)
    raw_update = gradient * row_factor[:, None] * lax.rsqrt(new_col)[None, :]
    update_total = lax.psum(jnp.sum(raw_update * raw_update), ("row", "col"))
    clip_scale = jnp.maximum(1.0, jnp.sqrt(update_total / cells))
    update = raw_update / clip_scale
    step_scale = rate * jnp.sqrt(param_total / cells)
    new_param = param - step_scale * update
    return (new_param, update, new_row, new_col, row_factor)


def solution(mesh):
    in_specs = (P("col", None), P(), P("row", "col"), P("row"), P("col"))
    out_specs = (P("row", "col"), P("row", "col"), P("row"), P("col"), P("row"))
    return jax.shard_map(body, mesh=mesh, in_specs=in_specs, out_specs=out_specs, check_vma=False)
```

profile of v0, /device:TPU:1, one launch (start us, length us, event | category | flops | bytes accessed | tf_op | source)
XLA Modules:
  0.0 359.5 jit_solution(14463881591033315878)
XLA Ops:
  0.6 3.3 copy.12
  3.9 2.9 copy.13
  6.8 11.9 %all-to-all-start = ((bf16[256,32,128]{2,0,1:T(8,128)(2,1)}), bf16[256,32,128]{2,0,1:T(8,128)(2,1)S(1)}, u32[]{:S(2)}, u32[]{:S(2)}) async-start(bf16[256,32,128]{2,0,1:T(8,128)(2,1)} %copy.13), calls=%async_computation | async-start | bytes 4194304 | tf_op jit(solution)/shard_map/all_to_all | solution.py:19
  18.7 0.0 copy-start.1
  18.7 2.7 multiply_reduce_fusion.1
  21.4 0.0 copy-done.1
  21.4 45.7 %all-to-all-done = bf16[256,32,128]{2,0,1:T(8,128)(2,1)S(1)} async-done(((bf16[256,32,128]{2,0,1:T(8,128)(2,1)}), bf16[256,32,128]{2,0,1:T(8,128)(2,1)S(1)}, u32[]{:S(2)}, u32[]{:S(2)}) %all-to-all-start) | async-done | bytes 2097184 | tf_op jit(solution)/shard_map/all_to_all | solution.py:19
  67.2 3.0 bitcast_select_fusion
  70.2 0.0 copy-start.3
  70.2 0.0 copy-start.4
  70.2 51.8 %scatter_custom_fusion = f32[4000,128]{1,0:T(8,128)S(1)} fusion(s32[8192]{0:T(1024)S(1)} %subtract_select_fusion, f32[8192,128]{1,0:T(8,128)} %bitcast_select_fusion, f32[]{:T(128)} %constant.13.clone.1), kind=kCustom, calls=%fused_computation.10 | custom fusion | flops 1048576 | bytes 2048512 | tf_op jit(solution)/shard_map/scatter-add | solution.py:25
  122.0 0.6 fusion.1
  122.7 112.7 %psum.36 = f32[4000]{0:T(1024)S(1)} all-reduce(f32[4000]{0:T(1024)S(1)} %get-tuple-element.5), channel_id=1, replica_groups=mesh['row'=8,'col'=32] {'col'}, use_global_device_ids=true, to_apply=%region_4.5 | all-reduce | flops 4000 | bytes 32000 | tf_op jit(solution)/shard_map/psum | solution.py:31
  235.4 0.0 copy-done.3
  235.4 0.6 fusion.7
  236.0 41.7 %all-reduce.1 = (f32[128]{0:T(128)S(1)}, f32[]{:T(128)}) all-reduce(f32[128]{0:T(128)S(1)} %get-tuple-element.6, f32[]{:T(128)} %get-tuple-element.15), channel_id=1, replica_groups=mesh['row'=8,'col'=32] {'row'}, use_global_device_ids=true, to_apply=%region_8.9 | all-reduce | flops 129 | bytes 1032 | tf_op jit(solution)/shard_map/psum | solution.py:29
  278.4 0.0 copy-start
  278.4 0.0 copy-done.4
  278.4 0.5 fusion.6
  278.9 2.3 multiply_reduce_fusion
  281.3 72.7 %all-reduce = (f32[]{:T(128)}, f32[]{:T(128)}) all-reduce(f32[]{:T(128)} %multiply_reduce_fusion, f32[]{:T(128)} %multiply_reduce_fusion.1), channel_id=1, replica_groups=mesh['row'=8,'col'=32] {'row','col'}, use_global_device_ids=true, to_apply=%region_10.11 | all-reduce | flops 2 | bytes 16 | tf_op jit(solution)/shard_map/psum | solution.py:36
  355.3 4.2 %multiply_subtract_fusion = (f32[4000,128]{1,0:T(8,128)}, f32[4000,128]{1,0:T(8,128)}) fusion(f32[4000,128]{1,0:T(8,128)} %param.7, f32[]{:T(128)S(6)} %mul_shard_map.3, f32[]{:T(128)S(6)} %max_shard_map.3, f32[128]{0:T(128)S(1)} %get-tuple-element.13, f32[4000,128]{1,0:T(8,128)S(1)} %scatter_custom_fusion, f32[4000]{0:T(1024)S(1)} %divide_rsqrt_fusion), kind=kLoop, calls=%fused_computation.2 | loop fusion | flops 2560000 | bytes 8208520 | tf_op jit(solution)/shard_map/sub | solution.py:40
  359.5 0.0 copy-done.2
  359.5 0.0 copy-done
  (4 shorter events, 0.0 us)
Async XLA Ops:
  6.8 60.4 %all-to-all-start = ((bf16[256,32,128]{2,0,1:T(8,128)(2,1)}), bf16[256,32,128]{2,0,1:T(8,128)(2,1)S(1)}, u32[]{:S(2)}, u32[]{:S(2)}) async-start(bf16[256,32,128]{2,0,1:T(8,128)(2,1)} %copy.13), calls=%async_computation | async-start | bytes 4194304 | tf_op jit(solution)/shard_map/all_to_all | solution.py:19
  18.7 2.7 copy-start.1
  70.2 165.2 %copy-start.3 = (f32[4000]{0:T(1024)S(1)}, f32[4000]{0:T(1024)}, u32[]{:S(2)}) copy-start(f32[4000]{0:T(1024)} %param.8) | copy-start | bytes 48004
  70.2 208.2 %copy-start.4 = (f32[128]{0:T(128)S(1)}, f32[128]{0:T(128)}, u32[]{:S(2)}) copy-start(f32[128]{0:T(128)} %param.9) | copy-start | bytes 1540
  236.0 123.6 %copy-start.2 = (f32[4000]{0:T(1024)}, f32[4000]{0:T(1024)S(1)}, u32[]{:S(2)}) copy-start(f32[4000]{0:T(1024)S(1)} %get-tuple-element.16) | copy-start | bytes 48004
  278.4 81.1 %copy-start = (f32[4000]{0:T(1024)}, f32[4000]{0:T(1024)S(1)}, u32[]{:S(2)}) copy-start(f32[4000]{0:T(1024)S(1)} %divide_rsqrt_fusion) | copy-start | bytes 48004
where the time goes:
time: 360 us
  blocking collectives  227 us (63%)
  other arithmetic  65.9 us (18%)
  waiting for transfers between devices  45.7 us (13%)
  starting transfers between devices  11.9 us (3%)
  local copies, waits for them, and re-layouts  6.2 us (2%)
    psum x1, blocking collectives, body(): row_total = lax.psum(row_local, 'col')  113 us
    psum x1, blocking collectives, body(): update_total = lax.psum(jnp.sum(raw_update * raw_update), ('row', 'col'))  72.7 us
    scatter-add x1, other arithmetic, body(): gradient = jax.ops.segment_sum(contrib, targets, num_segments=local_rows)  51.8 us
    all_to_all x1, waiting for transfers between devices, body(): lax.all_to_all(cotangent, 'col', split_axis=1, concat_axis=0, tiled=True)  45.7 us
    psum x1, blocking collectives, body(): col_total = lax.psum(col_local, 'row')  41.7 us
    all_to_all x1, starting transfers between devices, body(): lax.all_to_all(cotangent, 'col', split_axis=1, concat_axis=0, tiled=True)  11.9 us
  transfers between devices with their start and end apart: 1, of which 1 were waited for; matrix products, arithmetic and copies ran while one was open for 1% of the time, Pallas kernels for 0%

commit v1 on v0

v1 whole, which is shorter than its diff:
```python
import functools

import jax
import jax.numpy as jnp
from jax import lax
from jax.experimental import pallas as pl
from jax.experimental.pallas import tpu as pltpu
from jax.sharding import PartitionSpec as P

STEP = 100
DECAY = 1.0 - STEP ** (-0.8)
RATE = min(0.01, STEP ** (-0.5))
TINY = 1e-30
CAP = 64
BLOCK = 256
LANES = 128
NX = 4
ROW_TILE = 512
MESH = pl.DeviceIdType.MESH
F32 = jnp.float32
BF16 = jnp.bfloat16


def iota(shape, dim):
    return lax.broadcasted_iota(jnp.int32, shape, dim)


def dot(a, b):
    return jnp.dot(a, b, preferred_element_type=F32)


def dot_nt(a, b):
    return lax.dot_general(a, b, (((1,), (1,)), ((), ())), preferred_element_type=F32)


def order_of(n):
    return sorted(range(n), key=lambda d: (-min(d, n - d), d))


def step_kernel(
    n_row, n_col, local_rows, total_rows, total_cols,
    cot, ids, param, rowm, colm,
    raw_o, pv_o, r_o, nc_o, scal_o,
    cotv, posv, hiv, lov, slots, send, recv, oh, grad, sqt,
    col_recv, col_send, rs_send, rs_recv, ag_send, ag_recv, st_send, st_recv,
    cot_sem, param_sem, a2a_ssem, a2a_rsem, col_ssem, col_rsem,
    rs_ssem, rs_rsem, ag_ssem, ag_rsem, st_ssem, st_rsem,
):
    nz = n_col // NX
    rows_pad = n_col * LANES
    cells = float(total_rows) * float(total_cols)
    width = NX * LANES
    r = lax.axis_index("row")
    c = lax.axis_index("col")
    z = c // NX
    x = lax.rem(c, NX)
    order = order_of(nz)

    barrier = pltpu.get_barrier_semaphore()
    for k in range(1, n_col):
        pl.semaphore_signal(
            barrier, inc=1, device_id={"col": lax.rem(c + k, n_col)}, device_id_type=MESH
        )
    for k in range(1, n_row):
        pl.semaphore_signal(
            barrier, inc=1, device_id={"row": lax.rem(r + k, n_row)}, device_id_type=MESH
        )

    def cot_copy(j):
        zt = lax.rem(z + order[j], nz)
        return pltpu.make_async_copy(
            cot.at[:, pl.ds(pl.multiple_of(zt * width, width), width)], cotv.at[j], cot_sem.at[j]
        )

    for j in range(nz):
        cot_copy(j).start()
    param_copy = pltpu.make_async_copy(param, pv_o, param_sem)
    param_copy.start()

    local = ids[...] - r * local_rows
    inside = (local >= 0) & (local < local_rows)
    ones = jnp.where(inside, 1.0, 0.0).astype(BF16)
    before = jnp.where(iota((LANES, LANES), 0) < iota((LANES, LANES), 1), 1.0, 0.0).astype(BF16)
    count = dot(ones, before)
    total = dot(ones, jnp.ones((LANES, LANES), BF16))
    odd = lax.rem(iota(local.shape, 0), 2) == 1
    position = count + jnp.where(odd, pltpu.roll(total, 1, 0), 0.0)
    posv[...] = jnp.where(inside, position, -1000.0)
    tag = jnp.where(inside, local + 1, 0)
    hiv[...] = (tag >> 6).astype(F32)
    lov[...] = (tag & 63).astype(F32)

    slot_iota = iota((CAP, LANES), 0).astype(F32)

    def picks(row):
        return jnp.where(posv[pl.ds(row, 1), :] == slot_iota, 1.0, 0.0).astype(BF16)

    pick = jnp.concatenate([picks(2 * c), picks(2 * c + 1)], axis=1)

    def a2a_copy(j, dx):
        xt = lax.rem(x + dx, NX)
        zt = lax.rem(z + order[j], nz)
        return pltpu.make_async_remote_copy(
            src_ref=send.at[j, xt], dst_ref=recv.at[c],
            send_sem=a2a_ssem.at[j * NX + dx], recv_sem=a2a_rsem.at[c],
            device_id={"col": zt * NX + xt}, device_id_type=MESH,
        )

    def steps(j):
        return range(1, NX) if order[j] == 0 else range(NX)

    for j in range(nz):
        cot_copy(j).wait()
        packed = dot(pick, cotv[j]).astype(BF16)
        for k in range(NX):
            send[j, k] = packed[:, k * LANES:(k + 1) * LANES]
        if j == 0:
            pl.semaphore_wait(barrier, n_col + n_row - 2)
        for dx in steps(j):
            a2a_copy(j, dx).start()
        if order[j] == 0:
            recv[c] = send[j, x]

    pair_iota = iota((LANES, LANES), 0).astype(F32)
    first = iota((8, LANES), 0) == 0

    def slot_step(p, carry):
        found = jnp.zeros((8, LANES), F32)
        for h in range(4):
            row = 4 * p + h
            target = posv[pl.ds(row, 1), :] + float(CAP * (h // 2))
            onehot = jnp.where(target == pair_iota, 1.0, 0.0).astype(BF16)
            value = jnp.where(first, hiv[pl.ds(row, 1), :], lov[pl.ds(row, 1), :]).astype(BF16)
            found = found + dot_nt(value, onehot)
        slots[p] = jnp.broadcast_to(64.0 * found[0:1] + found[1:2] - 1.0, (8, LANES))
        return carry

    lax.fori_loop(0, n_col // 2, slot_step, 0)

    tile = 256
    tile_iota = iota((tile, LANES), 0).astype(F32)

    def onehot_step(i, carry):
        g = i // (rows_pad // tile)
        base = lax.rem(i, rows_pad // tile) * tile
        for h in range(2):
            wanted = slots[2 * g + h][0:1] - base.astype(F32)
            oh[g, pl.ds(pl.multiple_of(base, tile), tile), h * LANES:(h + 1) * LANES] = jnp.where(
                tile_iota == wanted, 1.0, 0.0
            ).astype(BF16)
        return carry

    lax.fori_loop(0, nz * (rows_pad // tile), onehot_step, 0)

    param_copy.wait()
    ptile = local_rows // 5

    def param_step(i, acc):
        block = pv_o[pl.ds(pl.multiple_of(i * ptile, 8), ptile), :]
        return acc + jnp.sum((block * block).reshape(ptile // 8, 8, LANES), axis=0)

    acc = lax.fori_loop(0, 5, param_step, jnp.zeros((8, LANES), F32))
    param_local = jnp.sum(jnp.sum(acc, axis=0, keepdims=True), axis=1, keepdims=True)

    mtile = min(ROW_TILE, rows_pad)
    for j in range(nz):
        zs = lax.rem(z + nz - order[j], nz)
        for dx in steps(j):
            xs = lax.rem(x + NX - dx, NX)
            src = zs * NX + xs
            pltpu.make_async_remote_copy(
                src_ref=send.at[j, 0], dst_ref=recv.at[src],
                send_sem=a2a_ssem.at[j * NX + dx], recv_sem=a2a_rsem.at[src],
                device_id={"col": src}, device_id_type=MESH,
            ).wait_recv()
        tokens = recv[pl.ds(zs * NX, NX)].reshape(NX * CAP, LANES)

        def grad_step(i, carry, j=j, zs=zs, tokens=tokens):
            rows = pl.ds(pl.multiple_of(i * mtile, mtile), mtile)
            part = dot(oh[zs, rows, :], tokens)
            grad[rows, :] = part if j == 0 else grad[rows, :] + part
            return carry

        lax.fori_loop(0, rows_pad // mtile, grad_step, 0)

    def col_step(i, acc):
        block = grad[pl.ds(pl.multiple_of(i * LANES, LANES), LANES), :]
        return acc + jnp.sum((block * block).reshape(LANES // 8, 8, LANES), axis=0)

    acc = lax.fori_loop(0, n_col, col_step, jnp.zeros((8, LANES), F32))
    col_send[0] = jnp.sum(acc, axis=0, keepdims=True)
    col_recv[r] = col_send[0]

    def over_row(src, dst, ssem, rsem):
        copies = [
            pltpu.make_async_remote_copy(
                src_ref=src.at[0], dst_ref=dst.at[r], send_sem=ssem.at[k - 1], recv_sem=rsem,
                device_id={"row": lax.rem(r + k, n_row)}, device_id_type=MESH,
            )
            for k in range(1, n_row)
        ]
        for copy in copies:
            copy.start()
        return copies

    def wait_all(buf, rsem, count):
        pltpu.make_async_copy(buf.at[pl.ds(0, count)], buf.at[pl.ds(0, count)], rsem).wait()

    col_copies = over_row(col_send, col_recv, col_ssem, col_rsem)

    def square_step(i, carry):
        block = grad[pl.ds(pl.multiple_of(i * LANES, LANES), LANES), :]
        turned = (block * block).T
        sqt[i] = turned
        rs_send[i, 0:1] = jnp.sum(turned, axis=0, keepdims=True)
        return carry

    lax.fori_loop(0, n_col, square_step, 0)

    wait_all(col_recv, col_rsem, n_row - 1)
    col_total = jnp.sum(col_recv[...], axis=0)
    new_col = DECAY * colm[...] + (1.0 - DECAY) * (col_total / float(total_rows) + TINY)
    nc_o[...] = new_col
    inverse_col = jnp.broadcast_to(1.0 / new_col, (LANES, LANES)).T

    def q_step(i, carry):
        rs_send[i, 1:2] = jnp.sum(sqt[i] * inverse_col, axis=0, keepdims=True)
        return carry

    lax.fori_loop(0, n_col, q_step, 0)

    def rs_copy(k):
        to = lax.rem(c + k, n_col)
        return pltpu.make_async_remote_copy(
            src_ref=rs_send.at[to], dst_ref=rs_recv.at[c], send_sem=rs_ssem.at[k], recv_sem=rs_rsem,
            device_id={"col": to}, device_id_type=MESH,
        )

    for k in range(1, n_col):
        rs_copy(k).start()
    rs_recv[c] = rs_send[c]
    wait_all(rs_recv, rs_rsem, n_col - 1)
    sums = jnp.sum(rs_recv[...], axis=0)

    lane = iota((1, LANES), 1)
    left = local_rows - c * LANES
    valid = lane < left
    new_row = DECAY * rowm[pl.ds(c, 1), :] + (1.0 - DECAY) * (sums[0:1] / float(total_cols) + TINY)
    row_sum = jnp.sum(jnp.where(valid, new_row, 0.0), axis=1, keepdims=True)
    raw_sum = jnp.sum(jnp.where(valid, sums[1:2] / new_row, 0.0), axis=1, keepdims=True)
    stats = jnp.where(lane == 0, row_sum, jnp.where(lane == 1, raw_sum, jnp.where(lane == 2, param_local, 0.0)))
    ag_send[0] = jnp.concatenate([new_row, stats], axis=0)
    ag_recv[c] = ag_send[0]

    def ag_copy(k):
        return pltpu.make_async_remote_copy(
            src_ref=ag_send.at[0], dst_ref=ag_recv.at[c], send_sem=ag_ssem.at[k], recv_sem=ag_rsem,
            device_id={"col": lax.rem(c + k, n_col)}, device_id_type=MESH,
        )

    for k in range(1, n_col):
        ag_copy(k).start()
    wait_all(ag_recv, ag_rsem, n_col - 1)
    gathered = ag_recv[...]
    st_send[0] = jnp.sum(gathered, axis=0)[1:2]
    st_recv[r] = st_send[0]
    st_copies = over_row(st_send, st_recv, st_ssem, st_rsem)

    rows_all = gathered[:, 0, :]
    r_o[...] = rows_all
    col_rsqrt = lax.rsqrt(new_col)
    full = local_rows // LANES
    rest = local_rows - full * LANES

    def scaled(i, size):
        factor = jnp.broadcast_to(lax.rsqrt(ag_recv[i][0:1]), (LANES, LANES)).T
        block = grad[pl.ds(pl.multiple_of(i * LANES, LANES), size), :]
        return block * factor[:size] * col_rsqrt

    def raw_step(i, carry):
        raw_o[pl.ds(pl.multiple_of(i * LANES, LANES), LANES), :] = scaled(i, LANES)
        return carry

    lax.fori_loop(0, full, raw_step, 0)
    if rest:
        raw_o[full * LANES:local_rows, :] = scaled(full, rest)

    wait_all(st_recv, st_rsem, n_row - 1)
    totals = jnp.sum(st_recv[...], axis=0)

    def pick_lane(k):
        return jnp.broadcast_to(
            jnp.sum(jnp.where(lane == k, totals, 0.0), axis=1, keepdims=True), (1, LANES)
        )

    mean_row = pick_lane(0) / float(total_rows)
    clip = jnp.maximum(1.0, jnp.sqrt(mean_row * pick_lane(1) / cells))
    root = jnp.sqrt(mean_row)
    step = RATE * jnp.sqrt(pick_lane(2) / cells)
    scal_o[0:1, :] = root / clip
    scal_o[1:2, :] = step
    scal_o[2:3, :] = root
    scal_o[3:8, :] = jnp.zeros((5, LANES), F32)

    for j in range(nz):
        for dx in steps(j):
            a2a_copy(j, dx).wait_send()
    for copy in col_copies + st_copies:
        copy.wait_send()
    for k in range(1, n_col):
        rs_copy(k).wait_send()
        ag_copy(k).wait_send()


def write_kernel(
    local_rows, raw, pv, rows, new_col, scal,
    np_o, up_o, nr_o, nc_o, rf_o,
    npv, upv, nrv, ncv, rfv, out_sem, small_sem,
):
    count = 10
    size = local_rows // count
    k = scal[0:1, :]
    step = scal[1:2, :]
    root = scal[2:3, :]
    copies = []
    for i in range(count):
        span = pl.ds(i * size, size)
        update = raw[span, :] * k
        upv[span, :] = update
        copies.append(pltpu.make_async_copy(upv.at[span], up_o.at[span], out_sem.at[0, i]))
        copies[-1].start()
        npv[span, :] = pv[span, :] - step * update
        copies.append(pltpu.make_async_copy(npv.at[span], np_o.at[span], out_sem.at[1, i]))
        copies[-1].start()
        if i == 0:
            values = rows[...]
            factor = lax.rsqrt(values) * root
            for j in range(pl.cdiv(local_rows, LANES)):
                n = min(LANES, local_rows - j * LANES)
                nrv[pl.ds(j * LANES, n)] = values[j, :n]
                rfv[pl.ds(j * LANES, n)] = factor[j, :n]
            ncv[...] = new_col[0, :]
            for q, (src, dst) in enumerate(((nrv, nr_o), (rfv, rf_o), (ncv, nc_o))):
                copies.append(pltpu.make_async_copy(src, dst, small_sem.at[q]))
                copies[-1].start()
    for copy in copies:
        copy.wait()


def body(n_row, n_col, cotangent, token_ids, param, row_moment, col_moment):
    local_rows, width = param.shape
    total_rows = local_rows * n_row
    total_cols = width * n_col
    rows_pad = n_col * LANES
    nz = n_col // NX
    vmem = pl.BlockSpec(memory_space=pltpu.VMEM)
    hbm = pl.BlockSpec(memory_space=pltpu.HBM)
    dma = pltpu.SemaphoreType.DMA

    ids = token_ids.reshape(n_col * BLOCK // LANES, LANES)
    rowm = jnp.pad(row_moment, (0, rows_pad - local_rows), constant_values=1.0).reshape(n_col, LANES)
    raw, pv, rows, new_col, scal = pl.pallas_call(
        functools.partial(step_kernel, n_row, n_col, local_rows, total_rows, total_cols),
        out_shape=(
            pltpu.VMEM((local_rows, LANES), F32),
            pltpu.VMEM((local_rows, LANES), F32),
            pltpu.VMEM((n_col, LANES), F32),
            pltpu.VMEM((1, LANES), F32),
            pltpu.VMEM((8, LANES), F32),
        ),
        in_specs=[hbm, vmem, hbm, vmem, vmem],
        out_specs=(vmem,) * 5,
        scratch_shapes=[
            pltpu.VMEM((nz, BLOCK, NX * LANES), BF16),
            pltpu.VMEM(ids.shape, F32),
            pltpu.VMEM(ids.shape, F32),
            pltpu.VMEM(ids.shape, F32),
            pltpu.VMEM((n_col // 2, 8, LANES), F32),
            pltpu.VMEM((nz, NX, CAP, LANES), BF16),
            pltpu.VMEM((n_col, CAP, LANES), BF16),
            pltpu.VMEM((nz, rows_pad, NX * CAP), BF16),
            pltpu.VMEM((rows_pad, LANES), F32),
            pltpu.VMEM((n_col, LANES, LANES), F32),
            pltpu.VMEM((n_row, 1, LANES), F32),
            pltpu.VMEM((1, 1, LANES), F32),
            pltpu.VMEM((n_col, 2, LANES), F32),
            pltpu.VMEM((n_col, 2, LANES), F32),
            pltpu.VMEM((1, 2, LANES), F32),
            pltpu.VMEM((n_col, 2, LANES), F32),
            pltpu.VMEM((1, 1, LANES), F32),
            pltpu.VMEM((n_row, 1, LANES), F32),
            dma((nz,)),
            dma,
            dma((n_col,)),
            dma((n_col,)),
            dma((n_row,)),
            dma,
            dma((n_col,)),
            dma,
            dma((n_col,)),
            dma,
            dma((n_row,)),
            dma,
        ],
        compiler_params=pltpu.CompilerParams(
            collective_id=0, has_side_effects=True, vmem_limit_bytes=44 * 1024 * 1024
        ),
        name="adafactor_step",
    )(cotangent, ids, param, rowm, col_moment.reshape(1, LANES))

    return pl.pallas_call(
        functools.partial(write_kernel, local_rows),
        out_shape=(
            jax.ShapeDtypeStruct((local_rows, LANES), F32),
            jax.ShapeDtypeStruct((local_rows, LANES), F32),
            jax.ShapeDtypeStruct((local_rows,), F32),
            jax.ShapeDtypeStruct((LANES,), F32),
            jax.ShapeDtypeStruct((local_rows,), F32),
        ),
        in_specs=[vmem] * 5,
        out_specs=(hbm,) * 5,
        scratch_shapes=[
            pltpu.VMEM((local_rows, LANES), F32),
            pltpu.VMEM((local_rows, LANES), F32),
            pltpu.VMEM((local_rows,), F32),
            pltpu.VMEM((LANES,), F32),
            pltpu.VMEM((local_rows,), F32),
            dma((2, 10)),
            dma((3,)),
        ],
        compiler_params=pltpu.CompilerParams(vmem_limit_bytes=16 * 1024 * 1024),
        name="adafactor_write",
    )(raw, pv, rows, new_col, scal)


def solution(mesh):
    n_row, n_col = mesh.shape["row"], mesh.shape["col"]
    in_specs = (P("col", None), P(), P("row", "col"), P("row"), P("col"))
    out_specs = (P("row", "col"), P("row", "col"), P("row"), P("col"), P("row"))
    return jax.shard_map(
        functools.partial(body, n_row, n_col),
        mesh=mesh, in_specs=in_specs, out_specs=out_specs, check_vma=False,
    )
```

time: 360 us -> 66.6 us (0.18)
  blocking collectives: 227 us -> 0 us
  other arithmetic: 65.9 us -> 0 us
  Pallas kernels: 0 us -> 60.4 us
  waiting for transfers between devices: 45.7 us -> 0 us
  starting transfers between devices: 11.9 us -> 0 us
    psum x3 -> x0, blocking collectives: 227 us -> none  [the longest x1 113 us: body(): row_total = lax.psum(row_local, 'col')]
    pallas_call x0 -> x2, Pallas kernels: none -> 60.4 us  [the longest x1 58.2 us: body(): pl.pallas_call(functools.partial(step_kernel, n_row, n_col, local_rows, t...]
    scatter-add x1 -> x0, other arithmetic: 51.8 us -> none  [body(): gradient = jax.ops.segment_sum(contrib, targets, num_segments=local_rows)]
    all_to_all x1 -> x0, waiting for transfers between devices: 45.7 us -> none  [body(): lax.all_to_all(cotangent, 'col', split_axis=1, concat_axis=0, tiled=True)]
    all_to_all x1 -> x0, starting transfers between devices: 11.9 us -> none  [body(): lax.all_to_all(cotangent, 'col', split_axis=1, concat_axis=0, tiled=True)]
    reduce_sum x4 -> x0, other arithmetic: 6.24 us -> none  [the longest x1 2.71 us: body(): param_total = lax.psum(jnp.sum(param * param), ('row', 'col'))]
    sub x1 -> x0, other arithmetic: 4.24 us -> none  [body(): new_param = param - step_scale * update]
  transfers between devices with their start and end apart: 1 -> 0, of which waited for: 1 -> 0; matrix products, arithmetic and copies ran while one was open for 1% -> 0% of each run, Pallas kernels for 0% -> 0%
where the time goes in v1:
time: 66.6 us; the launch traced here: 66.3 us
  Pallas kernels  60.4 us (91%)
  local copies, waits for them, and re-layouts  5.3 us (8%)
    pallas_call x1, Pallas kernels, body(): pl.pallas_call(functools.partial(step_kernel, n_row, n_col, local_rows, t...  58.2 us
    unnamed x8, local copies, waits for them, and re-layouts  4.58 us
    pallas_call x1, Pallas kernels, body(): pl.pallas_call(functools.partial(write_kernel, local_rows), out_shape=(ja...  2.2 us

profile of v1, /device:TPU:1, one launch (start us, length us, event | category | flops | bytes accessed | tf_op | source)
XLA Modules:
  0.0 66.3 jit_solution(16697578216073500900)
XLA Ops:
  0.6 0.7 %pad_bitcast_fusion.rowm = f32[32,128]{1,0:T(8,128)S(1)} fusion(f32[4000]{0:T(1024)} %param.9), kind=kLoop, calls=%fused_computation | loop fusion | bytes 32384 | tf_op jit(solution)/shard_map/reshape | solution.py:361
  1.4 0.0 copy-start
  1.4 1.6 %copy-done = bf16[256,4096]{1,0:T(8,128)(2,1)S(1)} copy-done((bf16[256,4096]{1,0:T(8,128)(2,1)S(1)}, bf16[256,4096]{1,0:T(8,128)(2,1)}, u32[]{:S(2)}) %copy-start) | copy-done | bytes 2097176
  2.9 0.0 copy-start.1
  2.9 1.6 %copy-done.1 = f32[4000,128]{1,0:T(8,128)S(1)} copy-done((f32[4000,128]{1,0:T(8,128)S(1)}, f32[4000,128]{1,0:T(8,128)}, u32[]{:S(2)}) %copy-start.1) | copy-done | bytes 2048024
  4.5 0.0 copy-start.2
  4.5 0.8 %copy-done.2 = s32[8192]{0:T(1024)S(1)} copy-done((s32[8192]{0:T(1024)S(1)}, s32[8192]{0:T(1024)}, u32[]{:S(2)}) %copy-start.2) | copy-done | bytes 32792
  5.3 0.0 copy-start.3
  5.3 0.7 copy-done.3
  5.9 58.2 %adafactor_step.1 = (f32[4000,128]{1,0:T(8,128)S(1)}, f32[4000,128]{1,0:T(8,128)S(1)}, f32[32,128]{1,0:T(8,128)S(1)}, f32[1,128]{1,0:T(1,128)S(1)}, f32[8,128]{1,0:T(8,128)S(1)}) custom-call(bf16[256,4096]{1,0:T(8,128)(2,1)S(1)} %copy-done, s32[64,128]{1,0:T(8,128)S(1)} %bitcast.4, f32[4000,128]{1,0:T(8,128)S(1)} %copy-done.1, ...), custom_call_target="tpu_custom_call" | custom-call | tf_op jit(solution)/shard_map/adafactor_step/pallas_call | solution.py:362
  64.1 2.2 %adafactor_write.1 = (f32[4000,128]{1,0:T(8,128)}, f32[4000,128]{1,0:T(8,128)}, f32[4000]{0:T(1024)}, f32[128]{0:T(128)}, f32[4000]{0:T(1024)}) custom-call(f32[4000,128]{1,0:T(8,128)S(1)} %get-tuple-element.10.raw, f32[4000,128]{1,0:T(8,128)S(1)} %get-tuple-element.11.pv, f32[32,128]{1,0:T(8,128)S(1)} %get-tuple-element.12.rows, ...), custom_call_target="tpu_custom_call" | custom-call | tf_op jit(solution)/shard_map/adafactor_write/pallas_call | solution.py:411
Async XLA Ops:
  1.4 1.6 %copy-start = (bf16[256,4096]{1,0:T(8,128)(2,1)S(1)}, bf16[256,4096]{1,0:T(8,128)(2,1)}, u32[]{:S(2)}) copy-start(bf16[256,4096]{1,0:T(8,128)(2,1)} %cot.1) | copy-start | bytes 6291460
  2.9 1.6 %copy-start.1 = (f32[4000,128]{1,0:T(8,128)S(1)}, f32[4000,128]{1,0:T(8,128)}, u32[]{:S(2)}) copy-start(f32[4000,128]{1,0:T(8,128)} %param.11) | copy-start | bytes 6144004
  4.5 0.8 %copy-start.2 = (s32[8192]{0:T(1024)S(1)}, s32[8192]{0:T(1024)}, u32[]{:S(2)}) copy-start(s32[8192]{0:T(1024)} %param.7) | copy-start | bytes 98308
  5.3 0.7 copy-start.3

commit v2 on v1

v2 whole, which is shorter than its diff:
```python
import functools

import jax
import jax.numpy as jnp
from jax import lax
from jax.experimental import pallas as pl
from jax.experimental.pallas import tpu as pltpu
from jax.sharding import PartitionSpec as P

STEP = 100
DECAY = 1.0 - STEP ** (-0.8)
RATE = min(0.01, STEP ** (-0.5))
TINY = 1e-30
CAP = 64
BLOCK = 256
LANES = 128
NX = 4
MESH = pl.DeviceIdType.MESH
F32 = jnp.float32
BF16 = jnp.bfloat16


def iota(shape, dim):
    return lax.broadcasted_iota(jnp.int32, shape, dim)


def dot(a, b):
    return jnp.dot(a, b, preferred_element_type=F32)


def dot_nt(a, b):
    return lax.dot_general(a, b, (((1,), (1,)), ((), ())), preferred_element_type=F32)


def order_of(nz):
    return sorted(range(nz), key=lambda d: (-min(d, nz - d), d))


def step_kernel(
    n_row, n_col, local_rows, total_rows, total_cols,
    cot, ids_hbm, param, rowm_hbm, colm_hbm,
    raw_o, pv_o, r_o, nc_o, scal_o,
    cotv, ids, rowm, moments, colm, posv, hiv, lov, high, low, send, recv, grad,
    col_send, col_recv, rs_send, rs_recv, zb_send, zb_recv, q_send, q_recv,
    ag_recv, sc_send, sc_recv, st_send, st_recv,
    in_sem, cot_sem, a2a_ssem, a2a_rsem, ssem, rsem,
):
    nz = n_col // NX
    cells = float(total_rows) * float(total_cols)
    width = NX * LANES
    r = lax.axis_index("row")
    c = lax.axis_index("col")
    z = c // NX
    x = lax.rem(c, NX)
    order = order_of(nz)

    barrier = pltpu.get_barrier_semaphore()
    for dz in order:
        for dx in (2, 1, 3, 0):
            if dz or dx:
                peer = lax.rem(z + dz, nz) * NX + lax.rem(x + dx, NX)
                pl.semaphore_signal(barrier, inc=1, device_id={"col": peer}, device_id_type=MESH)
    for k in range(1, n_row):
        pl.semaphore_signal(
            barrier, inc=1, device_id={"row": lax.rem(r + k, n_row)}, device_id_type=MESH
        )

    ids_copy = pltpu.make_async_copy(ids_hbm, ids, in_sem.at[0])
    ids_copy.start()

    def cot_copy(j):
        zt = lax.rem(z + order[j], nz)
        return pltpu.make_async_copy(
            cot.at[:, pl.ds(pl.multiple_of(zt * width, width), width)], cotv.at[j], cot_sem.at[j]
        )

    for j in range(nz):
        cot_copy(j).start()

    rowm_copy = pltpu.make_async_copy(rowm_hbm, rowm, in_sem.at[1])
    rowm_copy.start()
    colm_copy = pltpu.make_async_copy(colm_hbm, colm, in_sem.at[2])
    colm_copy.start()
    param_copy = pltpu.make_async_copy(param, pv_o, in_sem.at[3])
    param_copy.start()

    ids_copy.wait()
    local = ids[...] - r * local_rows
    inside = (local >= 0) & (local < local_rows)
    ones = jnp.where(inside, 1.0, 0.0).astype(BF16)
    before = jnp.where(iota((LANES, LANES), 0) < iota((LANES, LANES), 1), 1.0, 0.0).astype(BF16)
    count = dot(ones, before)
    total = dot(ones, jnp.ones((LANES, LANES), BF16))
    odd = lax.rem(iota(local.shape, 0), 2) == 1
    position = count + jnp.where(odd, pltpu.roll(total, 1, 0), 0.0)
    posv[...] = jnp.where(inside, position, -1000.0)
    hiv[...] = jnp.where(inside, (local >> 7) + 1, 0).astype(F32)
    lov[...] = jnp.where(inside, local & 127, 0).astype(F32)

    slot_iota = iota((CAP, LANES), 0).astype(F32)

    def picks(block):
        return jnp.concatenate(
            [
                jnp.where(posv[pl.ds(2 * block + h, 1), :] == slot_iota, 1.0, 0.0).astype(BF16)
                for h in range(2)
            ],
            axis=1,
        )

    pick = picks(c)

    def a2a_copy(j, dx):
        xt = lax.rem(x + dx, NX)
        zt = lax.rem(z + order[j], nz)
        return pltpu.make_async_remote_copy(
            src_ref=send.at[j, xt], dst_ref=recv.at[c],
            send_sem=a2a_ssem.at[j * NX + dx], recv_sem=a2a_rsem.at[c],
            device_id={"col": zt * NX + xt}, device_id_type=MESH,
        )

    def steps(j):
        return range(1, NX) if j == nz - 1 else range(NX)

    for j in range(nz):
        cot_copy(j).wait()
        packed = dot(pick, cotv[j]).astype(BF16)
        for k in range(NX):
            send[j, k] = packed[:, k * LANES:(k + 1) * LANES]
    recv[c] = send[nz - 1, x]
    pl.semaphore_wait(barrier, n_col + n_row - 2)
    for j in range(nz):
        for dx in steps(j):
            a2a_copy(j, dx).start()

    lane_iota = iota((CAP, LANES), 1).astype(F32)

    def slot_step(b, carry):
        g = b // NX
        span = pl.ds(pl.multiple_of(lax.rem(b, NX) * CAP, CAP), CAP)
        found = jnp.zeros((CAP, 2 * LANES), F32)
        both = picks(b)
        for h in range(2):
            row = pl.ds(2 * b + h, 1)
            values = jnp.concatenate(
                [
                    jnp.broadcast_to(hiv[row, :], (LANES, LANES)),
                    jnp.broadcast_to(lov[row, :], (LANES, LANES)),
                ],
                axis=0,
            ).astype(BF16)
            found = found + dot_nt(both[:, h * LANES:(h + 1) * LANES], values)
        high[g, span, :] = found[:, :LANES].astype(BF16)
        low[g, span, :] = jnp.where(found[:, LANES:] == lane_iota, 1.0, 0.0).astype(BF16)
        return carry

    lax.fori_loop(0, n_col, slot_step, 0, unroll=8)

    param_copy.wait()
    ptile = local_rows // 5

    def param_step(i, acc):
        block = pv_o[pl.ds(pl.multiple_of(i * ptile, 8), ptile), :]
        return acc + jnp.sum((block * block).reshape(ptile // 8, 8, LANES), axis=0)

    acc = lax.fori_loop(0, 5, param_step, jnp.zeros((8, LANES), F32))
    param_local = jnp.sum(jnp.sum(acc, axis=0, keepdims=True), axis=1, keepdims=True)

    grad[...] = jnp.zeros_like(grad)


    def wait_group(j, dxs):
        zs = lax.rem(z + nz - order[j], nz)
        for dx in dxs:
            src = zs * NX + lax.rem(x + NX - dx, NX)
            pltpu.make_async_remote_copy(
                src_ref=send.at[0, 0], dst_ref=recv.at[src],
                send_sem=a2a_ssem.at[0], recv_sem=a2a_rsem.at[src],
                device_id={"col": src}, device_id_type=MESH,
            ).wait_recv()
        return zs

    def parts(zs):
        turned = recv[pl.ds(zs * NX, NX)].reshape(NX * CAP, LANES).T
        hi, lo = high[zs], low[zs]
        zero = jnp.zeros_like(lo)
        for i in range(n_col // 2):
            onehot = jnp.concatenate(
                [jnp.where(hi == jnp.asarray(2 * i + h + 1, BF16), lo, zero) for h in range(2)], axis=1
            )
            part = dot(turned, onehot)
            for h in range(2):
                yield 2 * i + h, part[:, h * LANES:(h + 1) * LANES]

    for j in range(nz - 1):
        for i, part in parts(wait_group(j, steps(j))):
            grad[i] += part
    zs = wait_group(nz - 1, steps(nz - 1))
    acc = jnp.zeros((LANES, LANES), F32)
    for i, part in parts(zs):
        value = grad[i] + part
        grad[i] = value
        value = value * value
        acc = acc + value
        rs_send[i // nz, pl.ds(i % nz, 1), :] = jnp.sum(value, axis=0, keepdims=True)

    def exchange(src, dst, me, axis, q, count):
        copies = []
        for k in range(1, count):
            if axis == "row":
                device = {"row": lax.rem(r + k, n_row)}
                to = lax.rem(r + k, n_row)
            elif axis == "x":
                to = lax.rem(x + k, NX)
                device = {"col": z * NX + to}
            elif axis == "z":
                to = lax.rem(z + k, nz)
                device = {"col": to * NX + x}
            else:
                to = lax.rem(c + k, n_col)
                device = {"col": to}
            copies.append(
                pltpu.make_async_remote_copy(
                    src_ref=src.at[to] if src.shape[0] > 1 else src.at[0], dst_ref=dst.at[me],
                    send_sem=ssem.at[q, k], recv_sem=rsem.at[q],
                    device_id=device, device_id_type=MESH,
                )
            )
            copies[-1].start()
        return copies

    def wait_all(buf, q):
        rest = buf.at[pl.ds(0, buf.shape[0] - 1)]
        pltpu.make_async_copy(rest, rest, rsem.at[q]).wait()

    copies = exchange(rs_send, rs_recv, x, "x", 1, NX)
    col_send[0] = jnp.sum(acc.T, axis=0, keepdims=True)
    copies += exchange(col_send, col_recv, r, "row", 0, n_row)
    rs_recv[x] = rs_send[x]
    col_recv[r] = col_send[0]
    colm_copy.wait()
    rowm_copy.wait()
    for i in range(n_col):
        size = max(0, min(LANES, local_rows - i * LANES))
        if size < LANES:
            moments[pl.ds(i, 1), :] = jnp.ones((1, LANES), F32)
        if size:
            moments[i, :size] = rowm[pl.ds(i * LANES, size)]

    wait_all(rs_recv, 1)
    zb_send[0] = jnp.sum(rs_recv[...], axis=0)
    copies += exchange(zb_send, zb_recv, z, "z", 2, nz)
    zb_recv[z] = zb_send[0]

    wait_all(col_recv, 0)
    col_total = jnp.sum(col_recv[...], axis=0)
    new_col = DECAY * colm[...] + (1.0 - DECAY) * (col_total / float(total_rows) + TINY)
    nc_o[...] = new_col
    turned_col = jnp.broadcast_to(new_col, (LANES, LANES)).T
    inverse_col = 1.0 / turned_col
    for i in range(n_col):
        value = grad[i]
        q_send[i // nz, pl.ds(i % nz, 1), :] = jnp.sum(value * value * inverse_col, axis=0, keepdims=True)
    copies += exchange(q_send, q_recv, x, "x", 3, NX)
    q_recv[x] = q_send[x]

    wait_all(zb_recv, 2)
    row_total = jnp.sum(zb_recv[...], axis=0)
    moment = moments[pl.ds(pl.multiple_of(x * nz, nz), nz), :]
    new_row = DECAY * moment + (1.0 - DECAY) * (row_total / float(total_cols) + TINY)
    ag_recv[x] = new_row
    copies += exchange(ag_recv.at[pl.ds(x, 1)], ag_recv, x, "x", 4, NX)
    wait_all(q_recv, 3)
    row_id = x * (nz * LANES) + iota((nz, LANES), 0) * LANES + iota((nz, LANES), 1)
    valid = row_id < local_rows
    raw_part = jnp.sum(q_recv[...], axis=0) / new_row

    def total_of(value):
        return jnp.sum(jnp.sum(jnp.where(valid, value, 0.0), axis=0, keepdims=True), axis=1, keepdims=True)

    lane = iota((1, LANES), 1)
    row_sum = total_of(new_row) * (1.0 / nz)
    raw_sum = total_of(raw_part)
    sc_send[0] = jnp.where(
        lane == 0, row_sum, jnp.where(lane == 1, raw_sum, jnp.where(lane == 2, param_local, 0.0))
    )
    copies += exchange(sc_send, sc_recv, c, "col", 5, n_col)
    sc_recv[c] = sc_send[0]

    wait_all(ag_recv, 4)
    r_o[...] = ag_recv[...].reshape(n_col, LANES)
    col_rsqrt = lax.rsqrt(turned_col)

    def raw_chunk(i):
        size = min(LANES, local_rows - i * LANES)
        factor = lax.rsqrt(ag_recv[i // nz, pl.ds(i % nz, 1), :])
        raw_o[pl.ds(i * LANES, size), :] = (grad[i] * factor * col_rsqrt).T[:size]

    chunks = pl.cdiv(local_rows, LANES)
    for i in range(chunks // 2):
        raw_chunk(i)
    wait_all(sc_recv, 5)
    st_send[0] = jnp.sum(sc_recv[...], axis=0)
    copies += exchange(st_send, st_recv, r, "row", 6, n_row)
    st_recv[r] = st_send[0]
    for i in range(chunks // 2, chunks):
        raw_chunk(i)
    wait_all(st_recv, 6)
    totals = jnp.sum(st_recv[...], axis=0)

    def pick_lane(k):
        return jnp.broadcast_to(
            jnp.sum(jnp.where(lane == k, totals, 0.0), axis=1, keepdims=True), (1, LANES)
        )

    mean_row = pick_lane(0) / float(total_rows)
    clip = jnp.maximum(1.0, jnp.sqrt(mean_row * pick_lane(1) / cells))
    root = jnp.sqrt(mean_row)
    step = RATE * jnp.sqrt(pick_lane(2) / cells)
    scal_o[0:1, :] = root / clip
    scal_o[1:2, :] = step
    scal_o[2:3, :] = root
    scal_o[3:8, :] = jnp.zeros((5, LANES), F32)

    for j in range(nz):
        for dx in steps(j):
            a2a_copy(j, dx).wait_send()
    for copy in copies:
        copy.wait_send()


def write_kernel(
    local_rows, raw, pv, rows, new_col, scal,
    np_o, up_o, nr_o, nc_o, rf_o,
    npv, upv, nrv, ncv, rfv, out_sem, small_sem,
):
    count = 10
    size = local_rows // count
    k = scal[0:1, :]
    step = scal[1:2, :]
    root = scal[2:3, :]
    copies = []
    for i in range(count):
        span = pl.ds(i * size, size)
        update = raw[span, :] * k
        upv[span, :] = update
        copies.append(pltpu.make_async_copy(upv.at[span], up_o.at[span], out_sem.at[0, i]))
        copies[-1].start()
        npv[span, :] = pv[span, :] - step * update
        copies.append(pltpu.make_async_copy(npv.at[span], np_o.at[span], out_sem.at[1, i]))
        copies[-1].start()
        if i == 0:
            values = rows[...]
            factor = lax.rsqrt(values) * root
            for j in range(pl.cdiv(local_rows, LANES)):
                n = min(LANES, local_rows - j * LANES)
                nrv[pl.ds(j * LANES, n)] = values[j, :n]
                rfv[pl.ds(j * LANES, n)] = factor[j, :n]
            ncv[...] = new_col[0, :]
            for q, (src, dst) in enumerate(((nrv, nr_o), (rfv, rf_o), (ncv, nc_o))):
                copies.append(pltpu.make_async_copy(src, dst, small_sem.at[q]))
                copies[-1].start()
    for copy in copies:
        copy.wait()


def body(n_row, n_col, cotangent, token_ids, param, row_moment, col_moment):
    local_rows, width = param.shape
    total_rows = local_rows * n_row
    total_cols = width * n_col
    nz = n_col // NX
    vmem = pl.BlockSpec(memory_space=pltpu.VMEM)
    hbm = pl.BlockSpec(memory_space=pltpu.HBM)
    dma = pltpu.SemaphoreType.DMA

    ids_shape = (n_col * BLOCK // LANES, LANES)

    def stay(value):
        return pltpu.with_memory_space_constraint(value, pltpu.HBM)

    raw, pv, rows, new_col, scal = pl.pallas_call(
        functools.partial(step_kernel, n_row, n_col, local_rows, total_rows, total_cols),
        out_shape=(
            pltpu.VMEM((local_rows, LANES), F32),
            pltpu.VMEM((local_rows, LANES), F32),
            pltpu.VMEM((n_col, LANES), F32),
            pltpu.VMEM((1, LANES), F32),
            pltpu.VMEM((8, LANES), F32),
        ),
        in_specs=[hbm] * 5,
        out_specs=(vmem,) * 5,
        scratch_shapes=[
            pltpu.VMEM((nz, BLOCK, NX * LANES), BF16),
            pltpu.VMEM(ids_shape, jnp.int32),
            pltpu.VMEM((local_rows,), F32),
            pltpu.VMEM((n_col, LANES), F32),
            pltpu.VMEM((1, LANES), F32),
            pltpu.VMEM(ids_shape, F32),
            pltpu.VMEM(ids_shape, F32),
            pltpu.VMEM(ids_shape, F32),
            pltpu.VMEM((nz, NX * CAP, LANES), BF16),
            pltpu.VMEM((nz, NX * CAP, LANES), BF16),
            pltpu.VMEM((nz, NX, CAP, LANES), BF16),
            pltpu.VMEM((n_col, CAP, LANES), BF16),
            pltpu.VMEM((n_col, LANES, LANES), F32),
            pltpu.VMEM((1, 1, LANES), F32),
            pltpu.VMEM((n_row, 1, LANES), F32),
            pltpu.VMEM((NX, nz, LANES), F32),
            pltpu.VMEM((NX, nz, LANES), F32),
            pltpu.VMEM((1, nz, LANES), F32),
            pltpu.VMEM((nz, nz, LANES), F32),
            pltpu.VMEM((NX, nz, LANES), F32),
            pltpu.VMEM((NX, nz, LANES), F32),
            pltpu.VMEM((NX, nz, LANES), F32),
            pltpu.VMEM((1, 1, LANES), F32),
            pltpu.VMEM((n_col, 1, LANES), F32),
            pltpu.VMEM((1, 1, LANES), F32),
            pltpu.VMEM((n_row, 1, LANES), F32),
            dma((4,)),
            dma((nz,)),
            dma((n_col,)),
            dma((n_col,)),
            dma((7, max(n_col, n_row))),
            dma((7,)),
        ],
        compiler_params=pltpu.CompilerParams(
            collective_id=0, has_side_effects=True, vmem_limit_bytes=32 * 1024 * 1024
        ),
        name="adafactor_step",
    )(
        stay(cotangent), stay(token_ids.reshape(ids_shape)), stay(param), stay(row_moment),
        stay(col_moment.reshape(1, LANES)),
    )

    return pl.pallas_call(
        functools.partial(write_kernel, local_rows),
        out_shape=(
            jax.ShapeDtypeStruct((local_rows, LANES), F32),
            jax.ShapeDtypeStruct((local_rows, LANES), F32),
            jax.ShapeDtypeStruct((local_rows,), F32),
            jax.ShapeDtypeStruct((LANES,), F32),
            jax.ShapeDtypeStruct((local_rows,), F32),
        ),
        in_specs=[vmem] * 5,
        out_specs=(hbm,) * 5,
        scratch_shapes=[
            pltpu.VMEM((local_rows, LANES), F32),
            pltpu.VMEM((local_rows, LANES), F32),
            pltpu.VMEM((local_rows,), F32),
            pltpu.VMEM((LANES,), F32),
            pltpu.VMEM((local_rows,), F32),
            dma((2, 10)),
            dma((3,)),
        ],
        compiler_params=pltpu.CompilerParams(vmem_limit_bytes=16 * 1024 * 1024),
        name="adafactor_write",
    )(raw, pv, rows, new_col, scal)


def solution(mesh):
    n_row, n_col = mesh.shape["row"], mesh.shape["col"]
    in_specs = (P("col", None), P(), P("row", "col"), P("row"), P("col"))
    out_specs = (P("row", "col"), P("row", "col"), P("row"), P("col"), P("row"))
    return jax.shard_map(
        functools.partial(body, n_row, n_col),
        mesh=mesh, in_specs=in_specs, out_specs=out_specs, check_vma=False,
    )
```

time: 66.6 us -> 50.8 us (0.76)
  Pallas kernels: 60.4 us -> 50 us
  local copies, waits for them, and re-layouts: 5.3 us -> 0 us
    pallas_call x1, Pallas kernels: 58.2 us -> 47.8 us  [body(): pl.pallas_call(functools.partial(step_kernel, n_row, n_col, local_rows, t...]
    unnamed x8 -> x0, local copies, waits for them, and re-layouts: 4.58 us -> none
    reshape x1 -> x0, local copies, waits for them, and re-layouts: 0.72 us -> none  [body(): jnp.pad(row_moment, (0, rows_pad - local_rows), constant_values=1.0)]
where the time goes in v2:
time: 50.8 us; the launch traced here: 50.7 us
  Pallas kernels  50 us (98%)
  between operations  0.64 us (1%)
    pallas_call x1, Pallas kernels, body(): pl.pallas_call(functools.partial(step_kernel, n_row, n_col, local_rows, t...  47.8 us
    pallas_call x1, Pallas kernels, body(): pl.pallas_call(functools.partial(write_kernel, local_rows), out_shape=(ja...  2.2 us

profile of v2, /device:TPU:1, one launch (start us, length us, event | category | flops | bytes accessed | tf_op | source)
XLA Modules:
  0.0 50.7 jit_solution(12729502151379851279)
XLA Ops:
  0.6 47.8 %adafactor_step.1 = (f32[4000,128]{1,0:T(8,128)S(1)}, f32[4000,128]{1,0:T(8,128)S(1)}, f32[32,128]{1,0:T(8,128)S(1)}, f32[1,128]{1,0:T(1,128)S(1)}, f32[8,128]{1,0:T(8,128)S(1)}) custom-call(bf16[256,4096]{1,0:T(8,128)(2,1)} %cot.1, s32[64,128]{1,0:T(8,128)} %bitcast.2, f32[4000,128]{1,0:T(8,128)} %param.11, f32[4000]{0:T(1024)} %rowm_hbm.1, f32[1,128]{1,0:T(1,128)} %bitcast.3), custom_call_target="tpu_custom_call" | custom-call | tf_op jit(solution)/shard_map/adafactor_step/pallas_call | solution.py:381
  48.5 2.2 %adafactor_write.1 = (f32[4000,128]{1,0:T(8,128)}, f32[4000,128]{1,0:T(8,128)}, f32[4000]{0:T(1024)}, f32[128]{0:T(128)}, f32[4000]{0:T(1024)}) custom-call(f32[4000,128]{1,0:T(8,128)S(1)} %get-tuple-element.10.raw, f32[4000,128]{1,0:T(8,128)S(1)} %get-tuple-element.11.pv, f32[32,128]{1,0:T(8,128)S(1)} %get-tuple-element.12.rows, ...), custom_call_target="tpu_custom_call" | custom-call | tf_op jit(solution)/shard_map/adafactor_write/pallas_call | solution.py:435

commit v3 on v2

--- a/solution.py
+++ b/solution.py
@@ -15,6 +15,7 @@
 BLOCK = 256
 LANES = 128
 NX = 4
+GROUP = 4
 MESH = pl.DeviceIdType.MESH
 F32 = jnp.float32
 BF16 = jnp.bfloat16
@@ -33,7 +34,8 @@
 
 
 def order_of(nz):
-    return sorted(range(nz), key=lambda d: (-min(d, nz - d), d))
+    far = sorted(range(nz), key=lambda d: (-min(d, nz - d), d))
+    return [(dz, dx) for dx in (2, 1, 3, 0) for dz in far]
 
 
 def step_kernel(
@@ -41,7 +43,7 @@
     cot, ids_hbm, param, rowm_hbm, colm_hbm,
     raw_o, pv_o, r_o, nc_o, scal_o,
     cotv, ids, rowm, moments, colm, posv, hiv, lov, high, low, send, recv, grad,
-    col_send, col_recv, rs_send, rs_recv, zb_send, zb_recv, q_send, q_recv,
+    col_send, col_recv, rs_send, rs_recv, q_send, q_recv,
     ag_recv, sc_send, sc_recv, st_send, st_recv,
     in_sem, cot_sem, a2a_ssem, a2a_rsem, ssem, rsem,
 ):
@@ -55,11 +57,9 @@
     order = order_of(nz)
 
     barrier = pltpu.get_barrier_semaphore()
-    for dz in order:
-        for dx in (2, 1, 3, 0):
-            if dz or dx:
-                peer = lax.rem(z + dz, nz) * NX + lax.rem(x + dx, NX)
-                pl.semaphore_signal(barrier, inc=1, device_id={"col": peer}, device_id_type=MESH)
+    for dz, dx in order[:-1]:
+        peer = lax.rem(z + dz, nz) * NX + lax.rem(x + dx, NX)
+        pl.semaphore_signal(barrier, inc=1, device_id={"col": peer}, device_id_type=MESH)
     for k in range(1, n_row):
         pl.semaphore_signal(
             barrier, inc=1, device_id={"row": lax.rem(r + k, n_row)}, device_id_type=MESH
@@ -69,7 +69,7 @@
     ids_copy.start()
 
     def cot_copy(j):
-        zt = lax.rem(z + order[j], nz)
+        zt = lax.rem(z + j, nz)
         return pltpu.make_async_copy(
             cot.at[:, pl.ds(pl.multiple_of(zt * width, width), width)], cotv.at[j], cot_sem.at[j]
         )
@@ -110,34 +110,24 @@
 
     pick = picks(c)
 
-    def a2a_copy(j, dx):
-        xt = lax.rem(x + dx, NX)
-        zt = lax.rem(z + order[j], nz)
-        return pltpu.make_async_remote_copy(
-            src_ref=send.at[j, xt], dst_ref=recv.at[c],
-            send_sem=a2a_ssem.at[j * NX + dx], recv_sem=a2a_rsem.at[c],
-            device_id={"col": zt * NX + xt}, device_id_type=MESH,
-        )
-
-    def steps(j):
-        return range(1, NX) if j == nz - 1 else range(NX)
-
     for j in range(nz):
         cot_copy(j).wait()
         packed = dot(pick, cotv[j]).astype(BF16)
         for k in range(NX):
             send[j, k] = packed[:, k * LANES:(k + 1) * LANES]
-    recv[c] = send[nz - 1, x]
+    recv[c] = send[0, x]
     pl.semaphore_wait(barrier, n_col + n_row - 2)
-    for j in range(nz):
-        for dx in steps(j):
-            a2a_copy(j, dx).start()
+    for n, (dz, dx) in enumerate(order[:-1]):
+        xt = lax.rem(x + dx, NX)
+        pltpu.make_async_remote_copy(
+            src_ref=send.at[dz, xt], dst_ref=recv.at[c],
+            send_sem=a2a_ssem, recv_sem=a2a_rsem.at[n // GROUP],
+            device_id={"col": lax.rem(z + dz, nz) * NX + xt}, device_id_type=MESH,
+        ).start()
 
     lane_iota = iota((CAP, LANES), 1).astype(F32)
 
     def slot_step(b, carry):
-        g = b // NX
-        span = pl.ds(pl.multiple_of(lax.rem(b, NX) * CAP, CAP), CAP)
         found = jnp.zeros((CAP, 2 * LANES), F32)
         both = picks(b)
         for h in range(2):
@@ -150,8 +140,8 @@
                 axis=0,
             ).astype(BF16)
             found = found + dot_nt(both[:, h * LANES:(h + 1) * LANES], values)
-        high[g, span, :] = found[:, :LANES].astype(BF16)
-        low[g, span, :] = jnp.where(found[:, LANES:] == lane_iota, 1.0, 0.0).astype(BF16)
+        high[b] = found[:, :LANES].astype(BF16)
+        low[b] = jnp.where(found[:, LANES:] == lane_iota, 1.0, 0.0).astype(BF16)
         return carry
 
     lax.fori_loop(0, n_col, slot_step, 0, unroll=8)
@@ -169,20 +159,17 @@
     grad[...] = jnp.zeros_like(grad)
 
 
-    def wait_group(j, dxs):
-        zs = lax.rem(z + nz - order[j], nz)
-        for dx in dxs:
-            src = zs * NX + lax.rem(x + NX - dx, NX)
-            pltpu.make_async_remote_copy(
-                src_ref=send.at[0, 0], dst_ref=recv.at[src],
-                send_sem=a2a_ssem.at[0], recv_sem=a2a_rsem.at[src],
-                device_id={"col": src}, device_id_type=MESH,
-            ).wait_recv()
-        return zs
-
-    def parts(zs):
-        turned = recv[pl.ds(zs * NX, NX)].reshape(NX * CAP, LANES).T
-        hi, lo = high[zs], low[zs]
+    def parts(j):
+        members = order[j * GROUP:(j + 1) * GROUP]
+        arrivals = sum(1 for member in members if member != (0, 0))
+        landed = recv.at[pl.ds(0, arrivals)]
+        pltpu.make_async_copy(landed, landed, a2a_rsem.at[j]).wait()
+        sources = [
+            lax.rem(z + nz - dz, nz) * NX + lax.rem(x + NX - dx, NX) for dz, dx in members
+        ]
+        turned = jnp.concatenate([recv[src] for src in sources], axis=0).T
+        hi = jnp.concatenate([high[src] for src in sources], axis=0)
+        lo = jnp.concatenate([low[src] for src in sources], axis=0)
         zero = jnp.zeros_like(lo)
         for i in range(n_col // 2):
             onehot = jnp.concatenate(
@@ -192,51 +179,51 @@
             for h in range(2):
                 yield 2 * i + h, part[:, h * LANES:(h + 1) * LANES]
 
-    for j in range(nz - 1):
-        for i, part in parts(wait_group(j, steps(j))):
+    last = n_col // GROUP - 1
+    for j in range(last):
+        for i, part in parts(j):
             grad[i] += part
-    zs = wait_group(nz - 1, steps(nz - 1))
     acc = jnp.zeros((LANES, LANES), F32)
-    for i, part in parts(zs):
+    for i, part in parts(last):
         value = grad[i] + part
         grad[i] = value
         value = value * value
         acc = acc + value
         rs_send[i // nz, pl.ds(i % nz, 1), :] = jnp.sum(value, axis=0, keepdims=True)
 
-    def exchange(src, dst, me, axis, q, count):
-        copies = []
-        for k in range(1, count):
+    def exchange(src, dst, me, axis, q):
+        for k in range(1, {"row": n_row, "x": NX, "col": n_col}[axis]):
             if axis == "row":
                 device = {"row": lax.rem(r + k, n_row)}
-                to = lax.rem(r + k, n_row)
+                quarter = 0
             elif axis == "x":
-                to = lax.rem(x + k, NX)
-                device = {"col": z * NX + to}
-            elif axis == "z":
-                to = lax.rem(z + k, nz)
-                device = {"col": to * NX + x}
+                quarter = lax.rem(x + k, NX)
+                device = {"col": z * NX + quarter}
             else:
-                to = lax.rem(c + k, n_col)
-                device = {"col": to}
-            copies.append(
-                pltpu.make_async_remote_copy(
-                    src_ref=src.at[to] if src.shape[0] > 1 else src.at[0], dst_ref=dst.at[me],
-                    send_sem=ssem.at[q, k], recv_sem=rsem.at[q],
-                    device_id=device, device_id_type=MESH,
-                )
-            )
-            copies[-1].start()
-        return copies
+                dz, dx = order[k - 1]
+                quarter = lax.rem(x + dx, NX)
+                device = {"col": lax.rem(z + dz, nz) * NX + quarter}
+            pltpu.make_async_remote_copy(
+                src_ref=src.at[quarter if src.shape[0] > 1 else 0], dst_ref=dst.at[me],
+                send_sem=ssem.at[q], recv_sem=rsem.at[q],
+                device_id=device, device_id_type=MESH,
+            ).start()
 
     def wait_all(buf, q):
         rest = buf.at[pl.ds(0, buf.shape[0] - 1)]
         pltpu.make_async_copy(rest, rest, rsem.at[q]).wait()
 
-    copies = exchange(rs_send, rs_recv, x, "x", 1, NX)
+    def sent_all(buf, sem):
+        rest = buf.at[pl.ds(0, buf.shape[0] - 1)]
+        pltpu.make_async_remote_copy(
+            src_ref=rest, dst_ref=rest, send_sem=sem, recv_sem=sem,
+            device_id={"row": lax.rem(r + 1, n_row)}, device_id_type=MESH,
+        ).wait_send()
+
     col_send[0] = jnp.sum(acc.T, axis=0, keepdims=True)
-    copies += exchange(col_send, col_recv, r, "row", 0, n_row)
-    rs_recv[x] = rs_send[x]
+    exchange(col_send, col_recv, r, "row", 0)
+    exchange(rs_send, rs_recv, c, "col", 1)
+    rs_recv[c] = rs_send[x]
     col_recv[r] = col_send[0]
     colm_copy.wait()
     rowm_copy.wait()
@@ -247,11 +234,6 @@
         if size:
             moments[i, :size] = rowm[pl.ds(i * LANES, size)]
 
-    wait_all(rs_recv, 1)
-    zb_send[0] = jnp.sum(rs_recv[...], axis=0)
-    copies += exchange(zb_send, zb_recv, z, "z", 2, nz)
-    zb_recv[z] = zb_send[0]
-
     wait_all(col_recv, 0)
     col_total = jnp.sum(col_recv[...], axis=0)
     new_col = DECAY * colm[...] + (1.0 - DECAY) * (col_total / float(total_rows) + TINY)
@@ -261,16 +243,16 @@
     for i in range(n_col):
         value = grad[i]
         q_send[i // nz, pl.ds(i % nz, 1), :] = jnp.sum(value * value * inverse_col, axis=0, keepdims=True)
-    copies += exchange(q_send, q_recv, x, "x", 3, NX)
+    exchange(q_send, q_recv, x, "x", 2)
     q_recv[x] = q_send[x]
 
-    wait_all(zb_recv, 2)
-    row_total = jnp.sum(zb_recv[...], axis=0)
+    wait_all(rs_recv, 1)
+    row_total = jnp.sum(rs_recv[...], axis=0)
     moment = moments[pl.ds(pl.multiple_of(x * nz, nz), nz), :]
     new_row = DECAY * moment + (1.0 - DECAY) * (row_total / float(total_cols) + TINY)
     ag_recv[x] = new_row
-    copies += exchange(ag_recv.at[pl.ds(x, 1)], ag_recv, x, "x", 4, NX)
-    wait_all(q_recv, 3)
+    exchange(ag_recv.at[pl.ds(x, 1)], ag_recv, x, "x", 3)
+    wait_all(q_recv, 2)
     row_id = x * (nz * LANES) + iota((nz, LANES), 0) * LANES + iota((nz, LANES), 1)
     valid = row_id < local_rows
     raw_part = jnp.sum(q_recv[...], axis=0) / new_row
@@ -284,10 +266,10 @@
     sc_send[0] = jnp.where(
         lane == 0, row_sum, jnp.where(lane == 1, raw_sum, jnp.where(lane == 2, param_local, 0.0))
     )
-    copies += exchange(sc_send, sc_recv, c, "col", 5, n_col)
+    exchange(sc_send, sc_recv, c, "col", 4)
     sc_recv[c] = sc_send[0]
 
-    wait_all(ag_recv, 4)
+    wait_all(ag_recv, 3)
     r_o[...] = ag_recv[...].reshape(n_col, LANES)
     col_rsqrt = lax.rsqrt(turned_col)
 
@@ -299,13 +281,13 @@
     chunks = pl.cdiv(local_rows, LANES)
     for i in range(chunks // 2):
         raw_chunk(i)
-    wait_all(sc_recv, 5)
+    wait_all(sc_recv, 4)
     st_send[0] = jnp.sum(sc_recv[...], axis=0)
-    copies += exchange(st_send, st_recv, r, "row", 6, n_row)
+    exchange(st_send, st_recv, r, "row", 5)
     st_recv[r] = st_send[0]
     for i in range(chunks // 2, chunks):
         raw_chunk(i)
-    wait_all(st_recv, 6)
+    wait_all(st_recv, 5)
     totals = jnp.sum(st_recv[...], axis=0)
 
     def pick_lane(k):
@@ -322,11 +304,9 @@
     scal_o[2:3, :] = root
     scal_o[3:8, :] = jnp.zeros((5, LANES), F32)
 
-    for j in range(nz):
-        for dx in steps(j):
-            a2a_copy(j, dx).wait_send()
-    for copy in copies:
-        copy.wait_send()
+    sent_all(recv, a2a_ssem)
+    for q, buf in enumerate((col_recv, rs_recv, q_recv, ag_recv, sc_recv, st_recv)):
+        sent_all(buf, ssem.at[q])
 
 
 def write_kernel(
@@ -398,17 +378,15 @@
             pltpu.VMEM(ids_shape, F32),
             pltpu.VMEM(ids_shape, F32),
             pltpu.VMEM(ids_shape, F32),
-            pltpu.VMEM((nz, NX * CAP, LANES), BF16),
-            pltpu.VMEM((nz, NX * CAP, LANES), BF16),
+            pltpu.VMEM((n_col, CAP, LANES), BF16),
+            pltpu.VMEM((n_col, CAP, LANES), BF16),
             pltpu.VMEM((nz, NX, CAP, LANES), BF16),
             pltpu.VMEM((n_col, CAP, LANES), BF16),
             pltpu.VMEM((n_col, LANES, LANES), F32),
             pltpu.VMEM((1, 1, LANES), F32),
             pltpu.VMEM((n_row, 1, LANES), F32),
             pltpu.VMEM((NX, nz, LANES), F32),
-            pltpu.VMEM((NX, nz, LANES), F32),
-            pltpu.VMEM((1, nz, LANES), F32),
-            pltpu.VMEM((nz, nz, LANES), F32),
+            pltpu.VMEM((n_col, nz, LANES), F32),
             pltpu.VMEM((NX, nz, LANES), F32),
             pltpu.VMEM((NX, nz, LANES), F32),
             pltpu.VMEM((NX, nz, LANES), F32),
@@ -418,10 +396,10 @@
             pltpu.VMEM((n_row, 1, LANES), F32),
             dma((4,)),
             dma((nz,)),
-            dma((n_col,)),
-            dma((n_col,)),
-            dma((7, max(n_col, n_row))),
-            dma((7,)),
+            dma,
+            dma((n_col // GROUP,)),
+            dma((6,)),
+            dma((6,)),
         ],
         compiler_params=pltpu.CompilerParams(
             collective_id=0, has_side_effects=True, vmem_limit_bytes=32 * 1024 * 1024

time: 50.8 us -> 45.3 us (0.89)
  Pallas kernels: 50 us -> 44.6 us
    pallas_call x1, Pallas kernels: 47.8 us -> 42.4 us  [body(): pl.pallas_call(functools.partial(step_kernel, n_row, n_col, local_rows, t...]
where the time goes in v3:
time: 45.3 us
  Pallas kernels  44.6 us (98%)
  between operations  0.64 us (1%)
    pallas_call x1, Pallas kernels, body(): pl.pallas_call(functools.partial(step_kernel, n_row, n_col, local_rows, t...  42.4 us
    pallas_call x1, Pallas kernels, body(): pl.pallas_call(functools.partial(write_kernel, local_rows), out_shape=(ja...  2.2 us

profile of v3, /device:TPU:1, one launch (start us, length us, event | category | flops | bytes accessed | tf_op | source)
XLA Modules:
  0.0 45.3 jit_solution(1265482158228926445)
XLA Ops:
  0.6 42.4 %adafactor_step.1 = (f32[4000,128]{1,0:T(8,128)S(1)}, f32[4000,128]{1,0:T(8,128)S(1)}, f32[32,128]{1,0:T(8,128)S(1)}, f32[1,128]{1,0:T(1,128)S(1)}, f32[8,128]{1,0:T(8,128)S(1)}) custom-call(bf16[256,4096]{1,0:T(8,128)(2,1)} %cot.1, s32[64,128]{1,0:T(8,128)} %bitcast.2, f32[4000,128]{1,0:T(8,128)} %param.11, f32[4000]{0:T(1024)} %rowm_hbm.1, f32[1,128]{1,0:T(1,128)} %bitcast.3), custom_call_target="tpu_custom_call" | custom-call | tf_op jit(solution)/shard_map/adafactor_step/pallas_call | solution.py:361
  43.1 2.2 %adafactor_write.1 = (f32[4000,128]{1,0:T(8,128)}, f32[4000,128]{1,0:T(8,128)}, f32[4000]{0:T(1024)}, f32[128]{0:T(128)}, f32[4000]{0:T(1024)}) custom-call(f32[4000,128]{1,0:T(8,128)S(1)} %get-tuple-element.10.raw, f32[4000,128]{1,0:T(8,128)S(1)} %get-tuple-element.11.pv, f32[32,128]{1,0:T(8,128)S(1)} %get-tuple-element.12.rows, ...), custom_call_target="tpu_custom_call" | custom-call | tf_op jit(solution)/shard_map/adafactor_write/pallas_call | solution.py:413

commit v4 on v3

--- a/solution.py
+++ b/solution.py
@@ -44,7 +44,7 @@
     raw_o, pv_o, r_o, nc_o, scal_o,
     cotv, ids, rowm, moments, colm, posv, hiv, lov, high, low, send, recv, grad,
     col_send, col_recv, rs_send, rs_recv, q_send, q_recv,
-    ag_recv, sc_send, sc_recv, st_send, st_recv,
+    ag_recv, pair, chips,
     in_sem, cot_sem, a2a_ssem, a2a_rsem, ssem, rsem,
 ):
     nz = n_col // NX
@@ -54,6 +54,9 @@
     c = lax.axis_index("col")
     z = c // NX
     x = lax.rem(c, NX)
+    y = r // 2
+    core = lax.rem(r, 2)
+    ny = n_row // 2
     order = order_of(nz)
 
     barrier = pltpu.get_barrier_semaphore()
@@ -263,11 +266,26 @@
     lane = iota((1, LANES), 1)
     row_sum = total_of(new_row) * (1.0 / nz)
     raw_sum = total_of(raw_part)
-    sc_send[0] = jnp.where(
+    pair[core] = jnp.where(
         lane == 0, row_sum, jnp.where(lane == 1, raw_sum, jnp.where(lane == 2, param_local, 0.0))
     )
-    exchange(sc_send, sc_recv, c, "col", 4)
-    sc_recv[c] = sc_send[0]
+    pltpu.make_async_remote_copy(
+        src_ref=pair.at[core], dst_ref=pair.at[core], send_sem=ssem.at[4], recv_sem=rsem.at[4],
+        device_id={"row": 2 * y + 1 - core}, device_id_type=MESH,
+    ).start()
+    wait_all(pair, 4)
+    chip = c * ny + y
+    chips[chip] = pair[0] + pair[1]
+    for dz, dx in order:
+        for dy in range(ny - 1, -1, -1):
+            if dz or dx or dy:
+                to_row = 2 * lax.rem(y + dy, ny) + core
+                to_col = lax.rem(z + dz, nz) * NX + lax.rem(x + dx, NX)
+                pltpu.make_async_remote_copy(
+                    src_ref=chips.at[chip], dst_ref=chips.at[chip],
+                    send_sem=ssem.at[5], recv_sem=rsem.at[5],
+                    device_id={"row": to_row, "col": to_col}, device_id_type=MESH,
+                ).start()
 
     wait_all(ag_recv, 3)
     r_o[...] = ag_recv[...].reshape(n_col, LANES)
@@ -278,17 +296,10 @@
         factor = lax.rsqrt(ag_recv[i // nz, pl.ds(i % nz, 1), :])
         raw_o[pl.ds(i * LANES, size), :] = (grad[i] * factor * col_rsqrt).T[:size]
 
-    chunks = pl.cdiv(local_rows, LANES)
-    for i in range(chunks // 2):
+    for i in range(pl.cdiv(local_rows, LANES)):
         raw_chunk(i)
-    wait_all(sc_recv, 4)
-    st_send[0] = jnp.sum(sc_recv[...], axis=0)
-    exchange(st_send, st_recv, r, "row", 5)
-    st_recv[r] = st_send[0]
-    for i in range(chunks // 2, chunks):
-        raw_chunk(i)
-    wait_all(st_recv, 5)
-    totals = jnp.sum(st_recv[...], axis=0)
+    wait_all(chips, 5)
+    totals = jnp.sum(chips[...], axis=0)
 
     def pick_lane(k):
         return jnp.broadcast_to(
@@ -305,7 +316,7 @@
     scal_o[3:8, :] = jnp.zeros((5, LANES), F32)
 
     sent_all(recv, a2a_ssem)
-    for q, buf in enumerate((col_recv, rs_recv, q_recv, ag_recv, sc_recv, st_recv)):
+    for q, buf in enumerate((col_recv, rs_recv, q_recv, ag_recv, pair, chips)):
         sent_all(buf, ssem.at[q])
 
 
@@ -390,10 +401,8 @@
             pltpu.VMEM((NX, nz, LANES), F32),
             pltpu.VMEM((NX, nz, LANES), F32),
             pltpu.VMEM((NX, nz, LANES), F32),
-            pltpu.VMEM((1, 1, LANES), F32),
-            pltpu.VMEM((n_col, 1, LANES), F32),
-            pltpu.VMEM((1, 1, LANES), F32),
-            pltpu.VMEM((n_row, 1, LANES), F32),
+            pltpu.VMEM((2, 1, LANES), F32),
+            pltpu.VMEM((n_col * n_row // 2, 1, LANES), F32),
             dma((4,)),
             dma((nz,)),
             dma,

time: 45.3 us -> 43.8 us (0.967)
  Pallas kernels: 44.6 us -> 43.1 us
    pallas_call x1, Pallas kernels: 42.4 us -> 40.9 us  [body(): pl.pallas_call(functools.partial(step_kernel, n_row, n_col, local_rows, t...]
where the time goes in v4:
time: 43.8 us; the launch traced here: 43.7 us
  Pallas kernels  43.1 us (98%)
  between operations  0.64 us (1%)
    pallas_call x1, Pallas kernels, body(): pl.pallas_call(functools.partial(step_kernel, n_row, n_col, local_rows, t...  40.9 us
    pallas_call x1, Pallas kernels, body(): pl.pallas_call(functools.partial(write_kernel, local_rows), out_shape=(ja...  2.2 us

profile of v4, /device:TPU:1, one launch (start us, length us, event | category | flops | bytes accessed | tf_op | source)
XLA Modules:
  0.0 43.7 jit_solution(7603023981195295177)
XLA Ops:
  0.6 40.9 %adafactor_step.1 = (f32[4000,128]{1,0:T(8,128)S(1)}, f32[4000,128]{1,0:T(8,128)S(1)}, f32[32,128]{1,0:T(8,128)S(1)}, f32[1,128]{1,0:T(1,128)S(1)}, f32[8,128]{1,0:T(8,128)S(1)}) custom-call(bf16[256,4096]{1,0:T(8,128)(2,1)} %cot.1, s32[64,128]{1,0:T(8,128)} %bitcast.2, f32[4000,128]{1,0:T(8,128)} %param.11, f32[4000]{0:T(1024)} %rowm_hbm.1, f32[1,128]{1,0:T(1,128)} %bitcast.3), custom_call_target="tpu_custom_call" | custom-call | tf_op jit(solution)/shard_map/adafactor_step/pallas_call | solution.py:372
  41.5 2.2 %adafactor_write.1 = (f32[4000,128]{1,0:T(8,128)}, f32[4000,128]{1,0:T(8,128)}, f32[4000]{0:T(1024)}, f32[128]{0:T(128)}, f32[4000]{0:T(1024)}) custom-call(f32[4000,128]{1,0:T(8,128)S(1)} %get-tuple-element.10.raw, f32[4000,128]{1,0:T(8,128)S(1)} %get-tuple-element.11.pv, f32[32,128]{1,0:T(8,128)S(1)} %get-tuple-element.12.rows, ...), custom_call_target="tpu_custom_call" | custom-call | tf_op jit(solution)/shard_map/adafactor_write/pallas_call | solution.py:422

commit v5 on v4

--- a/solution.py
+++ b/solution.py
@@ -42,7 +42,7 @@
     n_row, n_col, local_rows, total_rows, total_cols,
     cot, ids_hbm, param, rowm_hbm, colm_hbm,
     raw_o, pv_o, r_o, nc_o, scal_o,
-    cotv, ids, rowm, moments, colm, posv, hiv, lov, high, low, send, recv, grad,
+    cotv, ids, rowm, moments, colm, posv, hiv, lov, high, low, ready, send, recv, grad,
     col_send, col_recv, rs_send, rs_recv, q_send, q_recv,
     ag_recv, pair, chips,
     in_sem, cot_sem, a2a_ssem, a2a_rsem, ssem, rsem,
@@ -74,7 +74,7 @@
     def cot_copy(j):
         zt = lax.rem(z + j, nz)
         return pltpu.make_async_copy(
-            cot.at[:, pl.ds(pl.multiple_of(zt * width, width), width)], cotv.at[j], cot_sem.at[j]
+            cot.at[:, pl.ds(pl.multiple_of(zt * width, width), width)], cotv.at[j], cot_sem
         )
 
     for j in range(nz):
@@ -113,8 +113,8 @@
 
     pick = picks(c)
 
+    pltpu.make_async_copy(cotv, cotv, cot_sem).wait()
     for j in range(nz):
-        cot_copy(j).wait()
         packed = dot(pick, cotv[j]).astype(BF16)
         for k in range(NX):
             send[j, k] = packed[:, k * LANES:(k + 1) * LANES]
@@ -162,27 +162,39 @@
     grad[...] = jnp.zeros_like(grad)
 
 
+    last = n_col // GROUP - 1
+    kept = range(max(0, last - 1), last + 1)
+
+    def sources(j):
+        return [
+            lax.rem(z + nz - dz, nz) * NX + lax.rem(x + NX - dx, NX)
+            for dz, dx in order[j * GROUP:(j + 1) * GROUP]
+        ]
+
+    def onehots(j):
+        hi = jnp.concatenate([high[src] for src in sources(j)], axis=0)
+        lo = jnp.concatenate([low[src] for src in sources(j)], axis=0)
+        zero = jnp.zeros_like(lo)
+        for i in range(n_col // 2):
+            yield jnp.concatenate(
+                [jnp.where(hi == jnp.asarray(2 * i + h + 1, BF16), lo, zero) for h in range(2)], axis=1
+            )
+
+    for j in kept:
+        for i, onehot in enumerate(onehots(j)):
+            ready[j - kept[0], i] = onehot
+
     def parts(j):
-        members = order[j * GROUP:(j + 1) * GROUP]
-        arrivals = sum(1 for member in members if member != (0, 0))
+        arrivals = sum(1 for member in order[j * GROUP:(j + 1) * GROUP] if member != (0, 0))
         landed = recv.at[pl.ds(0, arrivals)]
         pltpu.make_async_copy(landed, landed, a2a_rsem.at[j]).wait()
-        sources = [
-            lax.rem(z + nz - dz, nz) * NX + lax.rem(x + NX - dx, NX) for dz, dx in members
-        ]
-        turned = jnp.concatenate([recv[src] for src in sources], axis=0).T
-        hi = jnp.concatenate([high[src] for src in sources], axis=0)
-        lo = jnp.concatenate([low[src] for src in sources], axis=0)
-        zero = jnp.zeros_like(lo)
-        for i in range(n_col // 2):
-            onehot = jnp.concatenate(
-                [jnp.where(hi == jnp.asarray(2 * i + h + 1, BF16), lo, zero) for h in range(2)], axis=1
-            )
+        turned = jnp.concatenate([recv[src] for src in sources(j)], axis=0).T
+        made = (ready[j - kept[0], i] for i in range(n_col // 2)) if j in kept else onehots(j)
+        for i, onehot in enumerate(made):
             part = dot(turned, onehot)
             for h in range(2):
                 yield 2 * i + h, part[:, h * LANES:(h + 1) * LANES]
 
-    last = n_col // GROUP - 1
     for j in range(last):
         for i, part in parts(j):
             grad[i] += part
@@ -330,16 +342,14 @@
     k = scal[0:1, :]
     step = scal[1:2, :]
     root = scal[2:3, :]
-    copies = []
+    small = []
     for i in range(count):
         span = pl.ds(i * size, size)
         update = raw[span, :] * k
         upv[span, :] = update
-        copies.append(pltpu.make_async_copy(upv.at[span], up_o.at[span], out_sem.at[0, i]))
-        copies[-1].start()
+        pltpu.make_async_copy(upv.at[span], up_o.at[span], out_sem.at[0]).start()
         npv[span, :] = pv[span, :] - step * update
-        copies.append(pltpu.make_async_copy(npv.at[span], np_o.at[span], out_sem.at[1, i]))
-        copies[-1].start()
+        pltpu.make_async_copy(npv.at[span], np_o.at[span], out_sem.at[1]).start()
         if i == 0:
             values = rows[...]
             factor = lax.rsqrt(values) * root
@@ -349,9 +359,11 @@
                 rfv[pl.ds(j * LANES, n)] = factor[j, :n]
             ncv[...] = new_col[0, :]
             for q, (src, dst) in enumerate(((nrv, nr_o), (rfv, rf_o), (ncv, nc_o))):
-                copies.append(pltpu.make_async_copy(src, dst, small_sem.at[q]))
-                copies[-1].start()
-    for copy in copies:
+                small.append(pltpu.make_async_copy(src, dst, small_sem.at[q]))
+                small[-1].start()
+    pltpu.make_async_copy(upv, up_o, out_sem.at[0]).wait()
+    pltpu.make_async_copy(npv, np_o, out_sem.at[1]).wait()
+    for copy in small:
         copy.wait()
 
 
@@ -391,6 +403,7 @@
             pltpu.VMEM(ids_shape, F32),
             pltpu.VMEM((n_col, CAP, LANES), BF16),
             pltpu.VMEM((n_col, CAP, LANES), BF16),
+            pltpu.VMEM((2, n_col // 2, GROUP * CAP, 2 * LANES), BF16),
             pltpu.VMEM((nz, NX, CAP, LANES), BF16),
             pltpu.VMEM((n_col, CAP, LANES), BF16),
             pltpu.VMEM((n_col, LANES, LANES), F32),
@@ -404,7 +417,7 @@
             pltpu.VMEM((2, 1, LANES), F32),
             pltpu.VMEM((n_col * n_row // 2, 1, LANES), F32),
             dma((4,)),
-            dma((nz,)),
+            dma,
             dma,
             dma((n_col // GROUP,)),
             dma((6,)),
@@ -436,7 +449,7 @@
             pltpu.VMEM((local_rows,), F32),
             pltpu.VMEM((LANES,), F32),
             pltpu.VMEM((local_rows,), F32),
-            dma((2, 10)),
+            dma((2,)),
             dma((3,)),
         ],
         compiler_params=pltpu.CompilerParams(vmem_limit_bytes=16 * 1024 * 1024),

time: 43.8 us -> 43.6 us (level)
  no operation moved by 1% of the time
where the time goes in v5:
time: 43.6 us; the launch traced here: 43.5 us
  Pallas kernels  42.8 us (98%)
  between operations  0.64 us (1%)
    pallas_call x1, Pallas kernels, body(): pl.pallas_call(functools.partial(step_kernel, n_row, n_col, local_rows, t...  40.8 us
    pallas_call x1, Pallas kernels, body(): pl.pallas_call(functools.partial(write_kernel, local_rows), out_shape=(ja...  2.04 us

profile of v5, /device:TPU:1, one launch (start us, length us, event | category | flops | bytes accessed | tf_op | source)
XLA Modules:
  0.0 43.5 jit_solution(14203547725203621538)
XLA Ops:
  0.6 40.8 %adafactor_step.1 = (f32[4000,128]{1,0:T(8,128)S(1)}, f32[4000,128]{1,0:T(8,128)S(1)}, f32[32,128]{1,0:T(8,128)S(1)}, f32[1,128]{1,0:T(1,128)S(1)}, f32[8,128]{1,0:T(8,128)S(1)}) custom-call(bf16[256,4096]{1,0:T(8,128)(2,1)} %cot.1, s32[64,128]{1,0:T(8,128)} %bitcast.2, f32[4000,128]{1,0:T(8,128)} %param.11, f32[4000]{0:T(1024)} %rowm_hbm.1, f32[1,128]{1,0:T(1,128)} %bitcast.3), custom_call_target="tpu_custom_call" | custom-call | tf_op jit(solution)/shard_map/adafactor_step/pallas_call | solution.py:384
  41.4 2.0 %adafactor_write.1 = (f32[4000,128]{1,0:T(8,128)}, f32[4000,128]{1,0:T(8,128)}, f32[4000]{0:T(1024)}, f32[128]{0:T(128)}, f32[4000]{0:T(1024)}) custom-call(f32[4000,128]{1,0:T(8,128)S(1)} %get-tuple-element.10.raw, f32[4000,128]{1,0:T(8,128)S(1)} %get-tuple-element.11.pv, f32[32,128]{1,0:T(8,128)S(1)} %get-tuple-element.12.rows, ...), custom_call_target="tpu_custom_call" | custom-call | tf_op jit(solution)/shard_map/adafactor_write/pallas_call | solution.py:435

commit v6 on v5

--- a/solution.py
+++ b/solution.py
@@ -202,9 +202,7 @@
     for i, part in parts(last):
         value = grad[i] + part
         grad[i] = value
-        value = value * value
-        acc = acc + value
-        rs_send[i // nz, pl.ds(i % nz, 1), :] = jnp.sum(value, axis=0, keepdims=True)
+        acc = acc + value * value
 
     def exchange(src, dst, me, axis, q):
         for k in range(1, {"row": n_row, "x": NX, "col": n_col}[axis]):
@@ -237,6 +235,9 @@
 
     col_send[0] = jnp.sum(acc.T, axis=0, keepdims=True)
     exchange(col_send, col_recv, r, "row", 0)
+    for i in range(n_col):
+        value = grad[i]
+        rs_send[i // nz, pl.ds(i % nz, 1), :] = jnp.sum(value * value, axis=0, keepdims=True)
     exchange(rs_send, rs_recv, c, "col", 1)
     rs_recv[c] = rs_send[x]
     col_recv[r] = col_send[0]

time: 43.6 us -> 43.6 us (level)
  no operation moved by 1% of the time
where the time goes in v6:
time: 43.6 us; the launch traced here: 43.5 us
  Pallas kernels  42.8 us (98%)
  between operations  0.64 us (1%)
    pallas_call x1, Pallas kernels, body(): pl.pallas_call(functools.partial(step_kernel, n_row, n_col, local_rows, t...  40.8 us
    pallas_call x1, Pallas kernels, body(): pl.pallas_call(functools.partial(write_kernel, local_rows), out_shape=(ja...  2.04 us

profile of v6, /device:TPU:1, one launch (start us, length us, event | category | flops | bytes accessed | tf_op | source)
XLA Modules:
  0.0 43.5 jit_solution(6147021239601721720)
XLA Ops:
  0.6 40.8 %adafactor_step.1 = (f32[4000,128]{1,0:T(8,128)S(1)}, f32[4000,128]{1,0:T(8,128)S(1)}, f32[32,128]{1,0:T(8,128)S(1)}, f32[1,128]{1,0:T(1,128)S(1)}, f32[8,128]{1,0:T(8,128)S(1)}) custom-call(bf16[256,4096]{1,0:T(8,128)(2,1)} %cot.1, s32[64,128]{1,0:T(8,128)} %bitcast.2, f32[4000,128]{1,0:T(8,128)} %param.11, f32[4000]{0:T(1024)} %rowm_hbm.1, f32[1,128]{1,0:T(1,128)} %bitcast.3), custom_call_target="tpu_custom_call" | custom-call | tf_op jit(solution)/shard_map/adafactor_step/pallas_call | solution.py:385
  41.4 2.0 %adafactor_write.1 = (f32[4000,128]{1,0:T(8,128)}, f32[4000,128]{1,0:T(8,128)}, f32[4000]{0:T(1024)}, f32[128]{0:T(128)}, f32[4000]{0:T(1024)}) custom-call(f32[4000,128]{1,0:T(8,128)S(1)} %get-tuple-element.10.raw, f32[4000,128]{1,0:T(8,128)S(1)} %get-tuple-element.11.pv, f32[32,128]{1,0:T(8,128)S(1)} %get-tuple-element.12.rows, ...), custom_call_target="tpu_custom_call" | custom-call | tf_op jit(solution)/shard_map/adafactor_write/pallas_call | solution.py:436

commit v7 on v6

--- a/solution.py
+++ b/solution.py
@@ -35,7 +35,8 @@
 
 def order_of(nz):
     far = sorted(range(nz), key=lambda d: (-min(d, nz - d), d))
-    return [(dz, dx) for dx in (2, 1, 3, 0) for dz in far]
+    sides = [(dz, dx) for dz in far for dx in (1, 3)]
+    return [(dz, 2) for dz in far] + sides + [(dz, 0) for dz in far]
 
 
 def step_kernel(

time: 43.6 us -> 43.6 us (level)
  no operation moved by 1% of the time
where the time goes in v7:
time: 43.6 us; the launch traced here: 43.5 us
  Pallas kernels  42.9 us (98%)
  between operations  0.64 us (1%)
    pallas_call x1, Pallas kernels, body(): pl.pallas_call(functools.partial(step_kernel, n_row, n_col, local_rows, t...  40.8 us
    pallas_call x1, Pallas kernels, body(): pl.pallas_call(functools.partial(write_kernel, local_rows), out_shape=(ja...  2.04 us

profile of v7, /device:TPU:1, one launch (start us, length us, event | category | flops | bytes accessed | tf_op | source)
XLA Modules:
  0.0 43.5 jit_solution(14541588446495636080)
XLA Ops:
  0.6 40.8 %adafactor_step.1 = (f32[4000,128]{1,0:T(8,128)S(1)}, f32[4000,128]{1,0:T(8,128)S(1)}, f32[32,128]{1,0:T(8,128)S(1)}, f32[1,128]{1,0:T(1,128)S(1)}, f32[8,128]{1,0:T(8,128)S(1)}) custom-call(bf16[256,4096]{1,0:T(8,128)(2,1)} %cot.1, s32[64,128]{1,0:T(8,128)} %bitcast.2, f32[4000,128]{1,0:T(8,128)} %param.11, f32[4000]{0:T(1024)} %rowm_hbm.1, f32[1,128]{1,0:T(1,128)} %bitcast.3), custom_call_target="tpu_custom_call" | custom-call | tf_op jit(solution)/shard_map/adafactor_step/pallas_call | solution.py:386
  41.5 2.0 %adafactor_write.1 = (f32[4000,128]{1,0:T(8,128)}, f32[4000,128]{1,0:T(8,128)}, f32[4000]{0:T(1024)}, f32[128]{0:T(128)}, f32[4000]{0:T(1024)}) custom-call(f32[4000,128]{1,0:T(8,128)S(1)} %get-tuple-element.10.raw, f32[4000,128]{1,0:T(8,128)S(1)} %get-tuple-element.11.pv, f32[32,128]{1,0:T(8,128)S(1)} %get-tuple-element.12.rows, ...), custom_call_target="tpu_custom_call" | custom-call | tf_op jit(solution)/shard_map/adafactor_write/pallas_call | solution.py:437
